TPU v7x, 32 devices: a whole 2x2x4 slice. The times are simulated.
32 devices in a mesh: frame: 8 (over y, x, core), head: 4 (over z).
Axes of the slice: x: 2, y: 2, z: 4, core: 2. Of those that a mesh axis runs over, the one named last changes fastest.
Arguments:
- query_states: bfloat16 [4096, 1024], P('frame', 'head'), may hold values from -4.6 to 4.6
- key_states: bfloat16 [4096, 1024], P('frame', 'head'), may hold values from -4.6 to 4.6
- value_states: bfloat16 [4096, 1024], P('frame', 'head'), may hold values from -24 to 24
- out_weight: bfloat16 [1024, 5120], P('head'), may hold values from -0.1875 to 0.1875
- upstream: bfloat16 [4096, 5120], P('frame'), may hold values from -72 to 72
- tile_mask: int32 [16, 5], replicated, may hold values from 0 to 1, as said below
Outputs:
- attended: bfloat16 [4096, 1024], P('frame', 'head')
- projected: bfloat16 [4096, 5120], P('frame', 'head')
- grad_query: bfloat16 [4096, 1024], P('frame', 'head')
- grad_key: bfloat16 [4096, 1024], P('frame', 'head')
- grad_value: bfloat16 [4096, 1024], P('frame', 'head')
- gram_left: float32 [8, 16, 128, 128], P('head', 'frame')
- gram_right: float32 [8, 16, 320, 320], P('head', 'frame')
Inputs may be any that keep to these rules, and one draw needn't show every extreme that they name: `tile_mask`: in every row, column 2 (the query tile's own tile) is 1.
All inputs are finite; a program needn't handle non-finite values.
Results may differ from a plain program's by a relative error of at most 0.019.
Values may be sent and summed in bfloat16 or wider, within the bound.
A program may use at most 128 MiB of HBM per device.

v0:
```python
import math

import jax
import jax.numpy as jnp
from jax import lax
from jax.sharding import PartitionSpec as P

D = 5120
HD = 128
TILE = 256
TILES_DEV = 2
CB = 320


epsilon = 1e-06


def padded(shard, sides, width):
    for axis, dim in sides:
        devices, length = (lax.axis_size(axis), shard.shape[dim])
        up = [(i, (i + 1) % devices) for i in range(devices - 1)]
        down = [(j, i) for i, j in up]
        last = lax.slice_in_dim(shard, length - width, length, axis=dim)
        initial = lax.slice_in_dim(shard, 0, width, axis=dim)
        before = lax.ppermute(last, axis, up)
        after = lax.ppermute(initial, axis, down)
        shard = jnp.concatenate([before, shard, after], axis=dim)
    return shard


def from_behind(block, axis, distance):
    devices = range(lax.axis_size(axis))
    route = [(i - distance, i) for i in devices if i - distance in devices]
    return lax.ppermute(block, axis, route)


def tile_allowed(tile_mask, query_tiles, key_tiles):
    tile_count = tile_mask.shape[0]
    window = tile_mask.shape[1]
    reach_tiles = (window - 1) // 2
    row_hits = (query_tiles[:, None] == jnp.arange(tile_count, dtype=jnp.int32)[None, :]).astype(
        jnp.int32
    )
    picked = jnp.sum(row_hits[:, :, None] * tile_mask[None, :, :], axis=1)
    offsets = key_tiles[None, :] - query_tiles[:, None] + reach_tiles
    col_hits = offsets[:, :, None] == jnp.arange(window, dtype=jnp.int32)[None, None, :]
    chosen = jnp.sum(jnp.where(col_hits, picked[:, None, :], 0), axis=2)
    query_inside = (query_tiles >= 0) & (query_tiles < tile_count)
    key_inside = (key_tiles >= 0) & (key_tiles < tile_count)
    return (chosen > 0) & query_inside[:, None] & key_inside[None, :]


def masked_scores(queries, key_rows, query_tile, key_tile, tile_mask):
    scaling = 1.0 / math.sqrt(queries.shape[2])
    scores = (
        jnp.einsum("thd,shd->hts", queries, key_rows, preferred_element_type=jnp.float32) * scaling
    )
    heads_here = scores.shape[0]
    query_count = queries.shape[0] // TILE
    key_count = key_rows.shape[0] // TILE
    allowed = tile_allowed(
        tile_mask,
        query_tile + jnp.arange(query_count, dtype=jnp.int32),
        key_tile + jnp.arange(key_count, dtype=jnp.int32),
    )
    blocked = scores.reshape(heads_here, query_count, TILE, key_count, TILE)
    blocked = jnp.where(allowed[None, :, None, :, None], blocked, jnp.float32(-1e30))
    return blocked.reshape(scores.shape)


def log_total(scores):
    peak = jnp.max(scores, axis=2)
    return peak + jnp.log(jnp.sum(jnp.exp(scores - peak[:, :, None]), axis=2))


def local(query_states, key_states, value_states, out_weight, upstream, tile_mask):
    tok_rows = query_states.shape[0]
    heads_here = query_states.shape[1] // HD
    scaling = 1.0 / math.sqrt(HD)
    first_tile = lax.axis_index("frame") * TILES_DEV
    queries = query_states.reshape(tok_rows, heads_here, HD)
    stacked = jnp.stack([key_states, value_states])
    extended = padded(stacked, (("frame", 1),), tok_rows)
    keys_ext = extended[0].reshape(3 * tok_rows, heads_here, HD)
    values_ext = extended[1].reshape(3 * tok_rows, heads_here, HD)
    scores = masked_scores(queries, keys_ext, first_tile, first_tile - TILES_DEV, tile_mask)
    totals = log_total(scores)
    attention = jnp.exp(scores - totals[:, :, None])
    weights = attention.astype(jnp.bfloat16)
    attended3 = jnp.einsum(
        "hts,shd->thd", weights, values_ext, preferred_element_type=jnp.float32
    ).astype(jnp.bfloat16)
    attended = attended3.reshape(tok_rows, heads_here * HD)
    partial_value = jnp.dot(attended, out_weight, preferred_element_type=jnp.float32)
    projected = lax.psum_scatter(
        partial_value.astype(jnp.bfloat16), "head", scatter_dimension=1, tiled=True
    )
    grad_attended = lax.dot_general(
        upstream, out_weight, (((1,), (1,)), ((), ())), preferred_element_type=jnp.float32
    ).astype(jnp.bfloat16)
    grads3 = grad_attended.reshape(tok_rows, heads_here, HD)
    deltas = jnp.sum(grads3.astype(jnp.float32) * attended3.astype(jnp.float32), axis=2).T
    grad_probs = jnp.einsum("thd,shd->hts", grads3, values_ext, preferred_element_type=jnp.float32)
    grad_scores = (attention * (grad_probs - deltas[:, :, None])).astype(jnp.bfloat16)
    grad_query = (
        jnp.einsum("hts,shd->thd", grad_scores, keys_ext, preferred_element_type=jnp.float32)
        * scaling
    )
    grad_query = grad_query.astype(jnp.bfloat16).reshape(tok_rows, heads_here * HD)
    grad_keys = (
        jnp.einsum("hts,thd->shd", grad_scores, queries, preferred_element_type=jnp.float32)
        * scaling
    )
    grad_values = jnp.einsum("hts,thd->shd", weights, grads3, preferred_element_type=jnp.float32)
    pieces = jnp.stack([grad_keys, grad_values]).reshape(2, 3 * tok_rows, heads_here * HD)
    from_upper = from_behind(pieces[:, :tok_rows].astype(jnp.bfloat16), "frame", -1).astype(
        jnp.float32
    )
    from_lower = from_behind(pieces[:, 2 * tok_rows :].astype(jnp.bfloat16), "frame", 1).astype(
        jnp.float32
    )
    summed = pieces[:, tok_rows : 2 * tok_rows] + from_upper + from_lower
    grad_key = summed[0].astype(jnp.bfloat16)
    grad_value = summed[1].astype(jnp.bfloat16)
    local_cols = D // lax.axis_size("frame")
    column_share = lax.all_to_all(upstream, "frame", split_axis=1, concat_axis=0, tiled=True)
    grad_cols = lax.dot_general(
        column_share,
        lax.all_gather(attended, "frame", axis=0, tiled=True),
        (((0,), (0,)), ((), ())),
        preferred_element_type=jnp.float32,
    )
    blocks = grad_cols.reshape(local_cols // CB, CB, heads_here, HD)
    highest = lax.Precision.HIGHEST
    traces = jnp.einsum("bche,bche->hb", blocks, blocks, precision=highest)
    divisor = (traces + epsilon)[:, :, None, None]
    gram_left = HD * jnp.einsum("bche,bchf->hbef", blocks, blocks, precision=highest) / divisor
    gram_right = CB * jnp.einsum("bche,bdhe->hbcd", blocks, blocks, precision=highest) / divisor
    return (attended, projected, grad_query, grad_key, grad_value, gram_left, gram_right)


def solution(mesh):
    return jax.shard_map(
        local,
        mesh=mesh,
        in_specs=(
            P("frame", "head"),
            P("frame", "head"),
            P("frame", "head"),
            P("head", None),
            P("frame", None),
            P(),
        ),
        out_specs=(
            P("frame", "head"),
            P("frame", "head"),
            P("frame", "head"),
            P("frame", "head"),
            P("frame", "head"),
            P("head", "frame", None, None),
            P("head", "frame", None, None),
        ),
        check_vma=False,
    )
```

profile of v0, /device:TPU:9, one launch (start us, length us, event | category | flops | bytes accessed | tf_op | source)
XLA Modules:
  0.0 159.3 jit_solution(16737082752632377093)
XLA Ops:
  8.1 1.2 copy.82
  9.3 1.2 copy.81
  11.4 2.6 %collective-permute-start.1 = (bf16[2,512,256]{1,2,0:T(8,128)(2,1)}, bf16[2,512,256]{1,2,0:T(8,128)(2,1)}, u32[]{:S(2)}, u32[]{:S(2)}) collective-permute-start(bf16[2,512,256]{1,2,0:T(8,128)(2,1)} %pad_maximum_fusion.2), channel_id=1, source_target_pairs={{4,0},{8,4},{12,8},{16,12},{20,16},{24,20},{28,24},{5,1},{9,5},{13... | collective-permute-start | bytes 1572872 | tf_op jit(solution)/shard_map/ppermute | solution.py:26
  14.0 3.0 %collective-permute-start = (bf16[2,512,256]{1,2,0:T(8,128)(2,1)}, bf16[2,512,256]{1,2,0:T(8,128)(2,1)}, u32[]{:S(2)}, u32[]{:S(2)}) collective-permute-start(bf16[2,512,256]{1,2,0:T(8,128)(2,1)} %pad_maximum_fusion.2), channel_id=1, source_target_pairs={{0,4},{4,8},{8,12},{12,16},{16,20},{20,24},{24,28},{1,5},{5,9},{9,... | collective-permute-start | bytes 1572872 | tf_op jit(solution)/shard_map/ppermute | solution.py:25
  17.1 1.8 %copy.127 = bf16[512,256]{0,1:T(8,128)(2,1)} copy(bf16[512,256]{1,0:T(8,128)(2,1)} %param.6) | data formatting | bytes 524288 | tf_op jit(solution)/shard_map/reshape | solution.py:81
  20.8 1.8 %copy.83 = pred[512,1536]{0,1:T(8,128)(4,1)} copy(pred[512,1536]{1,0:T(8,128)(4,1)S(1)} %bitcast.72) | data formatting | bytes 1572864 | tf_op jit(solution)/shard_map/jit(_where)/broadcast_in_dim | solution.py:67
  22.6 4.1 %convolution_convert_fusion.2 = bf16[512,256]{0,1:T(8,128)(2,1)S(1)} fusion(bf16[512,5120]{1,0:T(8,128)(2,1)} %param.10, bf16[256,5120]{1,0:T(8,128)(2,1)S(1)} %copy-done), kind=kOutput, calls=%fused_computation.17 | convolution fusion | flops 1342308352 | bytes 8126464 | tf_op jit(solution)/shard_map/dot_general | solution.py:98
  26.8 1.4 pad_maximum_fusion.1
  28.4 1.6 fusion.14
  30.9 1.7 %copy-done.2 = f32[2,512,1536]{1,2,0:T(8,128)} copy-done((f32[2,512,1536]{1,2,0:T(8,128)}, f32[2,512,1536]{1,2,0:T(8,128)S(1)}, u32[]{:S(2)}) %copy-start.2) | copy-done | bytes 6291480
  32.6 1.9 %multiply_reduce_fusion.1 = (f32[512,2]{0,1:T(2,128)S(1)}, bf16[2,128,512]{2,1,0:T(8,128)(2,1)}) fusion(bf16[512,256]{0,1:T(8,128)(2,1)S(1)} %convolution_convert_fusion.2, bf16[1536,2,128]{0,2,1:T(8,128)(2,1)S(1)} %bitcast.62, f32[2,512,1536]{1,2,0:T(8,128)S(1)} %get-tuple-element.42, f32[2,512]{1,0:T(2,128)S(1)} %log_add_fusion), kind=kOutput, calls=%fused_computation.27 | convolution fusion | flops 406453248 | bytes 7610368 | tf_op jit(solution)/shard_map/hts,shd->thd/dot_general | solution.py:90
  34.6 4.9 %convolution_convert_fusion = bf16[512,5120]{1,0:T(8,128)(2,1)} fusion(bf16[512,256]{0,1:T(8,128)(2,1)} %bitcast.69, bf16[256,5120]{1,0:T(8,128)(2,1)S(1)} %copy-done), kind=kOutput, calls=%fused_computation | convolution fusion | flops 1344798720 | bytes 8126464 | tf_op jit(solution)/shard_map/dot_general | solution.py:94
  39.5 8.0 %copy.96 = bf16[512,5120]{0,1:T(8,128)(2,1)} copy(bf16[512,5120]{1,0:T(8,128)(2,1)} %param.10) | data formatting | bytes 10485760 | tf_op args[4]
  47.5 5.4 %all-to-all-start = ((bf16[512,8,640]{0,2,1:T(8,128)(2,1)}), bf16[512,8,640]{0,2,1:T(8,128)(2,1)}, u32[]{:S(2)}, u32[]{:S(2)}) async-start(bf16[512,8,640]{0,2,1:T(8,128)(2,1)} %bitcast.61), calls=%async_computation.1 | async-start | bytes 10485760 | tf_op jit(solution)/shard_map/all_to_all | solution.py:126
  52.9 4.3 %multiply_convert_fusion = bf16[2,512,1536]{1,2,0:T(8,128)(2,1)S(1)} fusion(f32[2,512,1536]{1,2,0:T(8,128)} %copy-done.2, bf16[512,2,128]{0,2,1:T(8,128)(2,1)S(1)} %bitcast.75, bf16[1536,2,128]{0,2,1:T(8,128)(2,1)S(1)} %bitcast.63, f32[2,512]{1,0:T(2,128)S(1)} %bitcast.84, f32[2,512]{1,0:T(2,128)S(1)} %log_add_fusion), kind=kOutput, calls=%fused_computation.2 | convolution fusion | flops 408944640 | bytes 10493952 | tf_op jit(solution)/shard_map/thd,shd->hts/dot_general | solution.py:103
  57.2 1.6 %copy-done.3 = bf16[2,512,1536]{1,2,0:T(8,128)(2,1)} copy-done((bf16[2,512,1536]{1,2,0:T(8,128)(2,1)}, bf16[2,512,1536]{1,2,0:T(8,128)(2,1)S(1)}, u32[]{:S(2)}) %copy-start.3) | copy-done | bytes 3145752
  58.8 2.3 %convolution_multiply_fusion = f32[2,1536,128]{1,2,0:T(8,128)} fusion(bf16[2,512,1536]{1,2,0:T(8,128)(2,1)S(1)} %multiply_convert_fusion, bf16[512,2,128]{0,2,1:T(8,128)(2,1)S(1)} %bitcast.82), kind=kOutput, calls=%fused_computation.10 | convolution fusion | flops 403046400 | bytes 4980736 | tf_op jit(solution)/shard_map/hts,thd->shd/dot_general | solution.py:111
  61.1 1.9 %copy.94 = f32[1,1536,256]{2,1,0:T(8,128)S(1)} copy(f32[1,1536,256]{1,2,0:T(8,128)} %bitcast.66) | data formatting | bytes 3145728 | tf_op jit(solution)/shard_map/stack | solution.py:115
  63.0 5.3 %fusion.8 = f32[2,128,1536]{2,1,0:T(8,128)} fusion(bf16[512,2,128]{0,2,1:T(8,128)(2,1)S(1)} %bitcast.76, f32[2,512,1536]{1,2,0:T(8,128)} %copy-done.2, f32[2,512]{1,0:T(2,128)S(1)} %log_add_fusion), kind=kOutput, calls=%fused_computation.24 | convolution fusion | flops 405798912 | bytes 8130560 | tf_op jit(solution)/shard_map/hts,thd->shd/dot_general | solution.py:114
  68.2 3.0 %copy.95 = f32[1,1536,256]{2,1,0:T(8,128)} copy(f32[1,1536,256]{1,2,0:T(8,128)} %bitcast.65) | data formatting | bytes 3145728 | tf_op jit(solution)/shard_map/stack | solution.py:115
  71.3 1.8 %fusion.1 = bf16[2,1536,256]{2,1,0:T(8,128)(2,1)S(1)} fusion(f32[1,1536,256]{2,1,0:T(8,128)} %copy.95, f32[1,1536,256]{2,1,0:T(8,128)S(1)} %copy.94), kind=kLoop, calls=%fused_computation.9 | loop fusion | flops 786432 | bytes 4718592 | tf_op jit(solution)/shard_map/convert.3
  73.1 1.1 fusion.12
  74.2 3.3 %collective-permute-start.3 = (bf16[2,512,256]{2,1,0:T(8,128)(2,1)}, bf16[2,512,256]{2,1,0:T(8,128)(2,1)S(1)}, u32[]{:S(2)}, u32[]{:S(2)}) collective-permute-start(bf16[2,512,256]{2,1,0:T(8,128)(2,1)} %get-tuple-element.36), channel_id=1, source_target_pairs={{0,4},{4,8},{8,12},{12,16},{16,20},{20,24},{24,28},{1,5},{5,9},{9,... | collective-permute-start | bytes 1572872 | tf_op jit(solution)/shard_map/ppermute | solution.py:34
  77.5 1.9 %collective-permute-start.2 = (bf16[2,512,256]{2,1,0:T(8,128)(2,1)}, bf16[2,512,256]{2,1,0:T(8,128)(2,1)}, u32[]{:S(2)}, u32[]{:S(2)}) collective-permute-start(bf16[2,512,256]{2,1,0:T(8,128)(2,1)} %get-tuple-element.35), channel_id=1, source_target_pairs={{4,0},{8,4},{12,8},{16,12},{20,16},{24,20},{28,24},{5,1},{9,5},{13... | collective-permute-start | bytes 1572872 | tf_op jit(solution)/shard_map/ppermute | solution.py:34
  80.3 2.5 %fusion.2 = bf16[2,128,512]{2,1,0:T(8,128)(2,1)S(1)} fusion(bf16[1536,2,128]{0,2,1:T(8,128)(2,1)S(1)} %bitcast.74, bf16[2,512,1536]{1,2,0:T(8,128)(2,1)} %copy-done.3), kind=kOutput, calls=%fused_computation.16 | convolution fusion | flops 402915328 | bytes 4194304 | tf_op jit(solution)/shard_map/hts,shd->thd/dot_general | solution.py:106
  83.6 37.6 %collective-permute-done.3 = bf16[2,512,256]{2,1,0:T(8,128)(2,1)S(1)} collective-permute-done((bf16[2,512,256]{2,1,0:T(8,128)(2,1)}, bf16[2,512,256]{2,1,0:T(8,128)(2,1)S(1)}, u32[]{:S(2)}, u32[]{:S(2)}) %collective-permute-start.3) | collective-permute-done | bytes 524320 | tf_op jit(solution)/shard_map/ppermute | solution.py:34
  121.2 7.9 %collective-permute-done.2 = bf16[2,512,256]{2,1,0:T(8,128)(2,1)} collective-permute-done((bf16[2,512,256]{2,1,0:T(8,128)(2,1)}, bf16[2,512,256]{2,1,0:T(8,128)(2,1)}, u32[]{:S(2)}, u32[]{:S(2)}) %collective-permute-start.2) | collective-permute-done | bytes 524320 | tf_op jit(solution)/shard_map/ppermute | solution.py:34
  129.0 1.4 fusion.7
  131.2 7.9 %copy.97 = bf16[8,512,640]{2,1,0:T(8,128)(2,1)} copy(bf16[8,512,640]{1,2,0:T(8,128)(2,1)} %bitcast.21) | data formatting | bytes 10485760 | tf_op jit(solution)/shard_map/all_to_all | solution.py:126
  139.1 4.9 %convolution_bitcast_fusion = f32[640,256]{0,1:T(8,128)S(1)} fusion(bf16[4096,256]{0,1:T(8,128)(2,1)} %all-gather.2.cloned.1.call-done, bf16[4096,640]{1,0:T(8,128)(2,1)} %bitcast.67), kind=kOutput, calls=%fused_computation.13 | convolution fusion | flops 1342177280 | bytes 7995392 | tf_op jit(solution)/shard_map/dot_general | solution.py:127
  146.7 2.2 %fusion.3 = f32[2,2,128,128]{3,2,1,0:T(8,128)} fusion(f32[2,320,2,128]{3,1,0,2:T(8,128)S(1)} %copy.99, f32[2,2]{1,0:T(2,128)S(1)} %broadcast_add_fusion), kind=kOutput, calls=%fused_computation.19 | convolution fusion | flops 251789312 | bytes 917520 | tf_op jit(solution)/shard_map/bche,bchf->hbef/dot_general | solution.py:137
  148.8 3.0 %multiply_divide_fusion = f32[2,2,320,320]{3,2,1,0:T(8,128)} fusion(f32[2,320,2,128]{3,1,0,2:T(8,128)S(1)} %copy.99, f32[2,2]{1,0:T(2,128)S(1)} %broadcast_add_fusion), kind=kOutput, calls=%fused_computation.11 | convolution fusion | flops 629964800 | bytes 2293776 | tf_op jit(solution)/shard_map/bche,bdhe->hbcd/dot_general | solution.py:138
  (63 shorter events, 9.1 us)
Async XLA Ops:
  8.0 14.6 %copy-start = (bf16[256,5120]{1,0:T(8,128)(2,1)S(1)}, bf16[256,5120]{1,0:T(8,128)(2,1)}, u32[]{:S(2)}) copy-start(bf16[256,5120]{1,0:T(8,128)(2,1)} %param.9) | copy-start | bytes 7864324
  8.0 131.1 %all-gather.2.cloned.1.call-start = ((), (), s32[]{:S(2)}) async-start(), calls=%async_computation.3 | async-start | bytes 2359296 | tf_op jit(solution)/shard_map/all_gather | solution.py:129
  9.3 11.1 %copy-start.9 = (bf16[512,256]{0,1:T(8,128)(2,1)}, bf16[512,256]{0,1:T(8,128)(2,1)S(1)}, u32[]{:S(2)}) copy-start(bf16[512,256]{0,1:T(8,128)(2,1)S(1)} %copy.82) | copy-start | bytes 786436
  10.5 9.9 %copy-start.11 = (bf16[512,256]{0,1:T(8,128)(2,1)}, bf16[512,256]{0,1:T(8,128)(2,1)S(1)}, u32[]{:S(2)}) copy-start(bf16[512,256]{0,1:T(8,128)(2,1)S(1)} %copy.81) | copy-start | bytes 786436
  11.4 15.4 %collective-permute-start.1 = (bf16[2,512,256]{1,2,0:T(8,128)(2,1)}, bf16[2,512,256]{1,2,0:T(8,128)(2,1)}, u32[]{:S(2)}, u32[]{:S(2)}) collective-permute-start(bf16[2,512,256]{1,2,0:T(8,128)(2,1)} %pad_maximum_fusion.2), channel_id=1, source_target_pairs={{4,0},{8,4},{12,8},{16,12},{20,16},{24,20},{28,24},{5,1},{9,5},{13... | collective-permute-start | bytes 1572872 | tf_op jit(solution)/shard_map/ppermute | solution.py:26
  14.0 12.8 %collective-permute-start = (bf16[2,512,256]{1,2,0:T(8,128)(2,1)}, bf16[2,512,256]{1,2,0:T(8,128)(2,1)}, u32[]{:S(2)}, u32[]{:S(2)}) collective-permute-start(bf16[2,512,256]{1,2,0:T(8,128)(2,1)} %pad_maximum_fusion.2), channel_id=1, source_target_pairs={{0,4},{4,8},{8,12},{12,16},{16,20},{20,24},{24,28},{1,5},{5,9},{9,... | collective-permute-start | bytes 1572872 | tf_op jit(solution)/shard_map/ppermute | solution.py:25
  22.6 4.2 %copy-start.10 = (bf16[512,256]{0,1:T(8,128)(2,1)S(1)}, bf16[512,256]{0,1:T(8,128)(2,1)}, u32[]{:S(2)}) copy-start(bf16[512,256]{0,1:T(8,128)(2,1)} %copy-done.9) | copy-start | bytes 786436
  22.6 4.2 %copy-start.12 = (bf16[512,256]{0,1:T(8,128)(2,1)S(1)}, bf16[512,256]{0,1:T(8,128)(2,1)}, u32[]{:S(2)}) copy-start(bf16[512,256]{0,1:T(8,128)(2,1)} %copy-done.11) | copy-start | bytes 786436
  26.7 4.2 %copy-start.7 = (bf16[512,256]{0,1:T(8,128)(2,1)}, bf16[512,256]{0,1:T(8,128)(2,1)S(1)}, u32[]{:S(2)}) copy-start(bf16[512,256]{0,1:T(8,128)(2,1)S(1)} %convolution_convert_fusion.2) | copy-start | bytes 786436
  26.7 1.6 %copy-start.13 = (bf16[512,256]{0,1:T(8,128)(2,1)S(1)}, bf16[512,256]{0,1:T(8,128)(2,1)}, u32[]{:S(2)}) copy-start(bf16[512,256]{0,1:T(8,128)(2,1)} %copy.127) | copy-start | bytes 786436
  26.8 1.6 %copy-start.15 = (pred[512,1536]{0,1:T(8,128)(4,1)S(1)}, pred[512,1536]{0,1:T(8,128)(4,1)}, u32[]{:S(2)}) copy-start(pred[512,1536]{0,1:T(8,128)(4,1)} %copy.83) | copy-start | bytes 2359300
  28.4 1.6 %copy-start.5 = (bf16[1,1536,256]{1,2,0:T(8,128)(2,1)}, bf16[1,1536,256]{1,2,0:T(8,128)(2,1)S(1)}, u32[]{:S(2)}) copy-start(bf16[1,1536,256]{1,2,0:T(8,128)(2,1)S(1)} %get-tuple-element.37) | copy-start | bytes 2359300
  30.0 2.7 %copy-start.2 = (f32[2,512,1536]{1,2,0:T(8,128)}, f32[2,512,1536]{1,2,0:T(8,128)S(1)}, u32[]{:S(2)}) copy-start(f32[2,512,1536]{1,2,0:T(8,128)S(1)} %get-tuple-element.42) | copy-start | bytes 18874372
  34.6 117.3 %reduce-scatter.2.cloned.1.call-start = ((), (), s32[]{:S(2)}) async-start(), calls=%async_computation.2 | async-start | bytes 6553600 | tf_op jit(solution)/shard_map/reduce_scatter | solution.py:95
  47.5 5.4 %copy-start.8 = (bf16[512,256]{0,1:T(8,128)(2,1)S(1)}, bf16[512,256]{0,1:T(8,128)(2,1)}, u32[]{:S(2)}) copy-start(bf16[512,256]{0,1:T(8,128)(2,1)} %copy-done.7) | copy-start | bytes 786436
  47.5 83.7 %all-to-all-start = ((bf16[512,8,640]{0,2,1:T(8,128)(2,1)}), bf16[512,8,640]{0,2,1:T(8,128)(2,1)}, u32[]{:S(2)}, u32[]{:S(2)}) async-start(bf16[512,8,640]{0,2,1:T(8,128)(2,1)} %bitcast.61), calls=%async_computation.1 | async-start | bytes 10485760 | tf_op jit(solution)/shard_map/all_to_all | solution.py:126
  52.9 5.9 %copy-start.14 = (bf16[512,256]{0,1:T(8,128)(2,1)S(1)}, bf16[512,256]{0,1:T(8,128)(2,1)}, u32[]{:S(2)}) copy-start(bf16[512,256]{0,1:T(8,128)(2,1)} %copy.127) | copy-start | bytes 786436
  57.2 1.6 %copy-start.3 = (bf16[2,512,1536]{1,2,0:T(8,128)(2,1)}, bf16[2,512,1536]{1,2,0:T(8,128)(2,1)S(1)}, u32[]{:S(2)}) copy-start(bf16[2,512,1536]{1,2,0:T(8,128)(2,1)S(1)} %multiply_convert_fusion) | copy-start | bytes 9437188
  71.3 8.1 %copy-start.4 = (bf16[2,128,512]{2,1,0:T(8,128)(2,1)S(1)}, bf16[2,128,512]{2,1,0:T(8,128)(2,1)}, u32[]{:S(2)}) copy-start(bf16[2,128,512]{2,1,0:T(8,128)(2,1)} %get-tuple-element.44) | copy-start | bytes 786436
  71.3 9.0 %copy-start.6 = (bf16[1,1536,256]{1,2,0:T(8,128)(2,1)S(1)}, bf16[1,1536,256]{1,2,0:T(8,128)(2,1)}, u32[]{:S(2)}) copy-start(bf16[1,1536,256]{1,2,0:T(8,128)(2,1)} %copy-done.5) | copy-start | bytes 2359300
  74.2 47.0 %collective-permute-start.3 = (bf16[2,512,256]{2,1,0:T(8,128)(2,1)}, bf16[2,512,256]{2,1,0:T(8,128)(2,1)S(1)}, u32[]{:S(2)}, u32[]{:S(2)}) collective-permute-start(bf16[2,512,256]{2,1,0:T(8,128)(2,1)} %get-tuple-element.36), channel_id=1, source_target_pairs={{0,4},{4,8},{8,12},{12,16},{16,20},{20,24},{24,28},{1,5},{5,9},{9,... | collective-permute-start | bytes 1572872 | tf_op jit(solution)/shard_map/ppermute | solution.py:34
  77.5 51.5 %collective-permute-start.2 = (bf16[2,512,256]{2,1,0:T(8,128)(2,1)}, bf16[2,512,256]{2,1,0:T(8,128)(2,1)}, u32[]{:S(2)}, u32[]{:S(2)}) collective-permute-start(bf16[2,512,256]{2,1,0:T(8,128)(2,1)} %get-tuple-element.35), channel_id=1, source_target_pairs={{4,0},{8,4},{12,8},{16,12},{20,16},{24,20},{28,24},{5,1},{9,5},{13... | collective-permute-start | bytes 1572872 | tf_op jit(solution)/shard_map/ppermute | solution.py:34
  146.7 5.1 %copy-start.1 = (bf16[256,5120]{1,0:T(8,128)(2,1)S(1)}, bf16[256,5120]{1,0:T(8,128)(2,1)}, u32[]{:S(2)}) copy-start(bf16[256,5120]{1,0:T(8,128)(2,1)} %param.9) | copy-start | bytes 7864324
Sparse Core Ops, SparseCore 0:
  34.7 36.1 all-gather.1
Sparse Core Ops, SparseCore 1:
  39.6 95.6 reduce-scatter.1
where the time goes:
time: 161 us; the launch traced here: 159 us
  waiting for transfers between devices  45.5 us (28%)
  local copies, waits for them, and re-layouts  36.9 us (23%)
  matrix products  36.8 us (23%)
  starting transfers between devices  16.3 us (10%)
  between operations  15.8 us (10%)
  other arithmetic  7.98 us (5%)
    ppermute x2, waiting for transfers between devices, from_behind(): return lax.ppermute(block, axis, route)  45.4 us
    unnamed x39, local copies, waits for them, and re-layouts  17 us
    all_to_all x1, local copies, waits for them, and re-layouts, local(): lax.all_to_all(upstream, 'frame', split_axis=1, concat_axis=0, tiled=True)  7.9 us
    all_to_all x1, starting transfers between devices, local(): lax.all_to_all(upstream, 'frame', split_axis=1, concat_axis=0, tiled=True)  5.35 us
    ppermute x2, starting transfers between devices, from_behind(): return lax.ppermute(block, axis, route)  5.26 us
    dot_general x1, matrix products, local(): jnp.einsum('hts,thd->shd', weights, grads3, preferred_element_type=jnp.fl...  5.26 us
    another operation x2, local copies, waits for them, and re-layouts, local(): jnp.stack([grad_keys, grad_values])  4.92 us
    dot_general x1, matrix products, local(): lax.dot_general(column_share, lax.all_gather(attended, 'frame', axis=0, t...  4.92 us
  transfers between devices with their start and end apart: 7, of which 2 were waited for; matrix products, arithmetic and copies ran while one was open for 43% of the time, Pallas kernels for 0%

commit v1 on v0

v1 whole, which is shorter than its diff:
```python
import functools
import math

import jax
import jax.numpy as jnp
from jax import lax
from jax.experimental import pallas as pl
from jax.experimental.pallas import tpu as pltpu
from jax.sharding import PartitionSpec as P

HD = 128
TILE = 256
CB = 320

epsilon = 1e-06
F32 = jnp.float32
BF16 = jnp.bfloat16
MESH = pl.DeviceIdType.MESH
NT = (((1,), (1,)), ((), ()))


def dot(a, b):
    return jnp.dot(a, b, preferred_element_type=F32)


def dot_nt(a, b):
    return lax.dot_general(a, b, NT, preferred_element_type=F32)


def kernel(
    nf, nh, tiles_all,
    q_hbm, k_hbm, v_hbm, w_hbm, wc_hbm, up_hbm, tm_ref,
    att_o, proj_o, dq_o, dk_o, dv_o, gl_o, gr_o,
    qv, kext, vext, wv, upb, wcols, attall, wts, attT, ga, gaT,
    kT, vT, dkacc, dvacc, ghs, ghr, outs, projv, pa, sa, pb, sb, rb,
    load_sem, up_sem, halo_s, halo_r, w_s, w_r, fw_s, fw_r, at_s, at_r,
    sa_s, sa_r, rb_s, rb_r, gh_s, gh_r, out_sem,
):
    f = lax.axis_index("frame")
    hd = lax.axis_index("head")
    core = lax.rem(f, 2)
    chip = lax.div(f, 2)
    chips = nf // 2
    sib = f + 1 - 2 * core
    tok, hw = qv.shape
    heads = hw // HD
    qt = tok // TILE
    win = tm_ref.shape[1]
    reach = (win - 1) // 2
    halo = reach * TILE
    span = win * TILE
    half = hw // 2
    cols = wcols.shape[2]
    cb = upb.shape[2]
    scale = 1.0 / math.sqrt(HD)

    barrier = pltpu.get_barrier_semaphore()
    for d in range(1, nf):
        pl.semaphore_signal(barrier, inc=1, device_id=(lax.rem(f + d, nf), hd), device_id_type=MESH)
    for d in range(1, nh):
        pl.semaphore_signal(barrier, inc=1, device_id=(f, lax.rem(hd + d, nh)), device_id_type=MESH)

    def w_block(j, rows):
        if cols % 128 == 0:
            return w_hbm.at[rows, pl.ds(pl.multiple_of(j * cols, 128), cols)]
        return wc_hbm.at[j, rows]

    def up_block(j):
        if cb % 128 == 0:
            return up_hbm.at[:, pl.ds(j * cb, cb)]
        return up_hbm.at[j]

    center = pl.ds(halo, tok)
    loads = [
        pltpu.make_async_copy(w_hbm, wv, load_sem.at[0]),
        pltpu.make_async_copy(k_hbm, kext.at[center], load_sem.at[1]),
        pltpu.make_async_copy(v_hbm, vext.at[center], load_sem.at[2]),
        pltpu.make_async_copy(q_hbm, qv, load_sem.at[3]),
        pltpu.make_async_copy(w_block(hd, pl.ds(0, hw)), wcols.at[hd], load_sem.at[4]),
    ]
    ups = [pltpu.make_async_copy(up_block(j), upb.at[j], up_sem.at[j]) for j in range(nf)]
    loads[0].start()
    for cp in ups:
        cp.start()
    for cp in loads[1:]:
        cp.start()

    pl.semaphore_wait(barrier, nf + nh - 2)

    def halo_copy(side, which):
        src = (k_hbm, v_hbm)[which]
        dst = (kext, vext)[which]
        rows = pl.ds(0, halo) if side == 0 else pl.ds(halo + tok, halo)
        part = pl.ds(tok - halo, halo) if side == 0 else pl.ds(0, halo)
        to = f + 1 if side == 0 else f - 1
        return pltpu.make_async_remote_copy(
            src_ref=src.at[part], dst_ref=dst.at[rows],
            send_sem=halo_s.at[side, which], recv_sem=halo_r.at[side, which],
            device_id=(to, hd), device_id_type=MESH)

    has_next = f < nf - 1
    has_prev = f > 0

    @pl.when(has_next)
    def _():
        for which in range(2):
            halo_copy(0, which).start()

    @pl.when(has_prev)
    def _():
        for which in range(2):
            halo_copy(1, which).start()

    my_rows = pl.ds(pl.multiple_of(core * half, half), half)
    w_copies = []
    for d in range(1, nh):
        j = lax.rem(hd + d, nh)
        cp = pltpu.make_async_remote_copy(
            src_ref=w_block(j, my_rows), dst_ref=wcols.at[hd, my_rows],
            send_sem=w_s.at[d], recv_sem=w_r.at[d],
            device_id=(f, j), device_id_type=MESH)
        cp.start()
        w_copies.append(cp)

    @pl.when(jnp.logical_not(has_prev))
    def _():
        kext[pl.ds(0, halo)] = jnp.zeros((halo, hw), BF16)
        vext[pl.ds(0, halo)] = jnp.zeros((halo, hw), BF16)

    @pl.when(jnp.logical_not(has_next))
    def _():
        kext[pl.ds(halo + tok, halo)] = jnp.zeros((halo, hw), BF16)
        vext[pl.ds(halo + tok, halo)] = jnp.zeros((halo, hw), BF16)

    loads[0].wait()
    acc = None
    for j in range(nf):
        ups[j].wait()
        part = dot_nt(wv[:, j * cb:(j + 1) * cb], upb[j])
        acc = part if acc is None else acc + part
    gaT[...] = acc.astype(BF16)
    ga[...] = acc.T.astype(BF16)
    for cp in loads[1:]:
        cp.wait()

    @pl.when(has_prev)
    def _():
        for which in range(2):
            halo_copy(0, which).wait_recv()

    @pl.when(has_next)
    def _():
        for which in range(2):
            halo_copy(1, which).wait_recv()

    kT[...] = kext[...].T
    vT[...] = vext[...].T

    def hcols(h):
        return pl.ds(h * HD, HD)

    for h in range(heads):
        for i in range(qt):
            rows = pl.ds(i * TILE, TILE)
            keys = pl.ds(i * TILE, span)
            s = dot_nt(kext[keys, hcols(h)], qv[rows, hcols(h)])
            parts = []
            tile = f * qt + i
            for o in range(win):
                b = tile + o - reach
                inside = jnp.where(jnp.logical_and(b >= 0, b < tiles_all), 1.0, 0.0)
                m = tm_ref[tile, o].astype(F32) * inside
                parts.append(s[o * TILE:(o + 1) * TILE] * (m * scale) + (m * 1e30 - 1e30))
            s = jnp.concatenate(parts, axis=0)
            p = jnp.exp(s - jnp.max(s, axis=0, keepdims=True))
            total = jnp.sum(p, axis=0, keepdims=True)
            wt = (p * (1.0 / total)).astype(BF16)
            wts[h * qt + i] = wt
            attT[hcols(h), rows] = dot(vT[hcols(h), keys], wt).astype(BF16)
    attall[hd] = attT[...].T

    att_out = pltpu.make_async_copy(attall.at[hd], att_o, out_sem.at[0])
    att_out.start()
    at_copies = []
    for d in range(1, nh):
        cp = pltpu.make_async_remote_copy(
            src_ref=attall.at[hd], dst_ref=attall.at[hd],
            send_sem=at_s.at[d], recv_sem=at_r.at[d],
            device_id=(f, lax.rem(hd + d, nh)), device_id_type=MESH)
        cp.start()
        at_copies.append(cp)

    order = [*range(1, chips), 0]
    sa_copies = {}
    for d in order:
        q = lax.rem(chip + d, chips)
        pa[d] = dot(attT[...], upb[2 * q + 1 - core]).astype(BF16)
        cp = pltpu.make_async_remote_copy(
            src_ref=pa.at[d], dst_ref=sa.at[d], send_sem=sa_s.at[d], recv_sem=sa_r.at[d],
            device_id=(sib, hd), device_id_type=MESH)
        cp.start()
        sa_copies[d] = cp
    rb_copies = {}
    for d in order:
        q = lax.rem(chip + d, chips)
        part = dot(attT[...], upb[2 * q + core])
        sa_copies[d].wait_recv()
        part = part + sa[d].astype(F32)
        if d == 0:
            pb[...] = part
        else:
            sb[d] = part.astype(BF16)
            cp = pltpu.make_async_remote_copy(
                src_ref=sb.at[d], dst_ref=rb.at[d], send_sem=rb_s.at[d], recv_sem=rb_r.at[d],
                device_id=(2 * q + core, hd), device_id_type=MESH)
            cp.start()
            rb_copies[d] = cp

    dkacc[...] = jnp.zeros_like(dkacc)
    dvacc[...] = jnp.zeros_like(dvacc)
    for h in range(heads):
        for i in range(qt):
            rows = pl.ds(i * TILE, TILE)
            keys = pl.ds(i * TILE, span)
            wt = wts[h * qt + i]
            g = dot_nt(vext[keys, hcols(h)], ga[rows, hcols(h)])
            delta = jnp.sum(
                gaT[hcols(h), rows].astype(F32) * attT[hcols(h), rows].astype(F32),
                axis=0, keepdims=True)
            ds = (wt.astype(F32) * (g - delta)).astype(BF16)
            dqT = dot(kT[hcols(h), keys], ds) * scale
            outs[0, rows, hcols(h)] = dqT.T.astype(BF16)
            dkacc[keys, hcols(h)] += dot(ds, qv[rows, hcols(h)])
            dvacc[keys, hcols(h)] += dot(wt, ga[rows, hcols(h)])

    dq_out = pltpu.make_async_copy(outs.at[0], dq_o, out_sem.at[1])
    dq_out.start()

    def gh_copy(side):
        to = f + 1 if side == 0 else f - 1
        return pltpu.make_async_remote_copy(
            src_ref=ghs.at[side], dst_ref=ghr.at[side],
            send_sem=gh_s.at[side], recv_sem=gh_r.at[side],
            device_id=(to, hd), device_id_type=MESH)

    upper = pl.ds(halo + tok, halo)
    lower = pl.ds(0, halo)
    ghs[0, 0] = (dkacc[upper] * scale).astype(BF16)
    ghs[0, 1] = dvacc[upper].astype(BF16)
    ghs[1, 0] = (dkacc[lower] * scale).astype(BF16)
    ghs[1, 1] = dvacc[lower].astype(BF16)

    @pl.when(has_next)
    def _():
        gh_copy(0).start()

    @pl.when(has_prev)
    def _():
        gh_copy(1).start()

    @pl.when(jnp.logical_not(has_prev))
    def _():
        ghr[0] = jnp.zeros(ghr.shape[1:], BF16)

    @pl.when(jnp.logical_not(has_next))
    def _():
        ghr[1] = jnp.zeros(ghr.shape[1:], BF16)

    fw_copies = []
    for d in range(1, nh):
        w_copies[d - 1].wait_recv()
        s = lax.rem(hd + nh - d, nh)
        cp = pltpu.make_async_remote_copy(
            src_ref=wcols.at[s, my_rows], dst_ref=wcols.at[s, my_rows],
            send_sem=fw_s.at[d], recv_sem=fw_r.at[d],
            device_id=(sib, hd), device_id_type=MESH)
        cp.start()
        fw_copies.append(cp)

    @pl.when(has_prev)
    def _():
        gh_copy(0).wait_recv()

    @pl.when(has_next)
    def _():
        gh_copy(1).wait_recv()

    first, last = slice(0, halo), slice(tok - halo, tok)
    for which, (full, factor) in enumerate(((dkacc, scale), (dvacc, 1.0))):
        full[pl.ds(halo, halo)] += ghr[0, which].astype(F32) * (1.0 / factor)
        full[pl.ds(tok, halo)] += ghr[1, which].astype(F32) * (1.0 / factor)
        outs[1 + which] = (full[center] * factor).astype(BF16)
    dk_out = pltpu.make_async_copy(outs.at[1], dk_o, out_sem.at[2])
    dv_out = pltpu.make_async_copy(outs.at[2], dv_o, out_sem.at[3])
    dk_out.start()
    dv_out.start()

    grad = pb[...]
    for d in range(1, chips):
        rb_copies[d].wait_recv()
        grad = grad + rb[d].astype(F32)
    for h in range(heads):
        for n in range(cb // CB):
            block = grad[h * HD:(h + 1) * HD, n * CB:(n + 1) * CB]
            trace = jnp.sum(jnp.sum(block * block, axis=0, keepdims=True), axis=1, keepdims=True)
            inverse = 1.0 / (trace + epsilon)
            small = block.astype(BF16)
            gl_o[h, n] = dot_nt(small, small) * (inverse * HD)
            gr_o[h, n] = dot(block.T.astype(BF16), small) * (inverse * CB)

    at_copies_all = at_copies
    acc = dot(attall[hd], wcols[hd])
    for d in range(1, nh):
        s = lax.rem(hd + nh - d, nh)
        at_copies_all[d - 1].wait_recv()
        fw_copies[d - 1].wait_recv()
        acc = acc + dot(attall[s], wcols[s])
    projv[...] = acc.astype(BF16)
    proj_out = pltpu.make_async_copy(projv, proj_o, out_sem.at[4])
    proj_out.start()

    for cp in (*w_copies, *fw_copies, *at_copies, *sa_copies.values(), *rb_copies.values()):
        cp.wait_send()

    @pl.when(has_next)
    def _():
        for which in range(2):
            halo_copy(0, which).wait_send()
        gh_copy(0).wait_send()

    @pl.when(has_prev)
    def _():
        for which in range(2):
            halo_copy(1, which).wait_send()
        gh_copy(1).wait_send()

    for cp in (att_out, dq_out, dk_out, dv_out, proj_out):
        cp.wait()


def local(query_states, key_states, value_states, out_weight, upstream, tile_mask):
    nf = lax.axis_size("frame")
    nh = lax.axis_size("head")
    tok, hw = query_states.shape
    heads = hw // HD
    width = out_weight.shape[1]
    cols = width // nh
    cb = width // nf
    chips = nf // 2
    win = tile_mask.shape[1]
    reach = (win - 1) // 2
    halo = reach * TILE
    ext = tok + 2 * halo
    w_in = out_weight
    if cols % 128:
        w_in = out_weight.reshape(hw, nh, cols).transpose(1, 0, 2)
    up_in = upstream
    if cb % 128:
        up_in = upstream.reshape(tok, nf, cb).transpose(1, 0, 2)
    anywhere = pl.BlockSpec(memory_space=pl.ANY)
    vmem = pl.BlockSpec(memory_space=pltpu.VMEM)
    dma = pltpu.SemaphoreType.DMA
    return pl.pallas_call(
        functools.partial(kernel, nf, nh, tile_mask.shape[0]),
        out_shape=(
            jax.ShapeDtypeStruct((tok, hw), BF16),
            jax.ShapeDtypeStruct((tok, cols), BF16),
            jax.ShapeDtypeStruct((tok, hw), BF16),
            jax.ShapeDtypeStruct((tok, hw), BF16),
            jax.ShapeDtypeStruct((tok, hw), BF16),
            jax.ShapeDtypeStruct((heads, cb // CB, HD, HD), F32),
            jax.ShapeDtypeStruct((heads, cb // CB, CB, CB), F32),
        ),
        in_specs=[anywhere] * 6 + [pl.BlockSpec(memory_space=pltpu.SMEM)],
        out_specs=(anywhere,) * 5 + (vmem, vmem),
        scratch_shapes=[
            pltpu.VMEM((tok, hw), BF16),
            pltpu.VMEM((ext, hw), BF16),
            pltpu.VMEM((ext, hw), BF16),
            pltpu.VMEM((hw, width), BF16),
            pltpu.VMEM((nf, tok, cb), BF16),
            pltpu.VMEM((nh, hw, cols), BF16),
            pltpu.VMEM((nh, tok, hw), BF16),
            pltpu.VMEM((heads * (tok // TILE), win * TILE, TILE), BF16),
            pltpu.VMEM((hw, tok), BF16),
            pltpu.VMEM((tok, hw), BF16),
            pltpu.VMEM((hw, tok), BF16),
            pltpu.VMEM((hw, ext), BF16),
            pltpu.VMEM((hw, ext), BF16),
            pltpu.VMEM((ext, hw), F32),
            pltpu.VMEM((ext, hw), F32),
            pltpu.VMEM((2, 2, halo, hw), BF16),
            pltpu.VMEM((2, 2, halo, hw), BF16),
            pltpu.VMEM((3, tok, hw), BF16),
            pltpu.VMEM((tok, cols), BF16),
            pltpu.VMEM((chips, hw, cb), BF16),
            pltpu.VMEM((chips, hw, cb), BF16),
            pltpu.VMEM((hw, cb), F32),
            pltpu.VMEM((chips, hw, cb), BF16),
            pltpu.VMEM((chips, hw, cb), BF16),
            dma((5,)),
            dma((nf,)),
            dma((2, 2)), dma((2, 2)),
            dma((nh,)), dma((nh,)),
            dma((nh,)), dma((nh,)),
            dma((nh,)), dma((nh,)),
            dma((chips,)), dma((chips,)),
            dma((chips,)), dma((chips,)),
            dma((2,)), dma((2,)),
            dma((5,)),
        ],
        compiler_params=pltpu.CompilerParams(
            collective_id=0, has_side_effects=True, vmem_limit_bytes=56 * 1024 * 1024),
    )(query_states, key_states, value_states, out_weight, w_in, up_in, tile_mask)


def solution(mesh):
    return jax.shard_map(
        local,
        mesh=mesh,
        in_specs=(
            P("frame", "head"),
            P("frame", "head"),
            P("frame", "head"),
            P("head", None),
            P("frame", None),
            P(),
        ),
        out_specs=(
            P("frame", "head"),
            P("frame", "head"),
            P("frame", "head"),
            P("frame", "head"),
            P("frame", "head"),
            P("head", "frame", None, None),
            P("head", "frame", None, None),
        ),
        check_vma=False,
    )
```

time: 161 us -> 71 us (0.44)
  Pallas kernels: 0 us -> 60.1 us
  waiting for transfers between devices: 45.5 us -> 0 us
  matrix products: 36.8 us -> 0 us
  local copies, waits for them, and re-layouts: 36.9 us -> 9.79 us
  starting transfers between devices: 16.3 us -> 0 us
  between operations: 15.8 us -> 0.66 us
  other arithmetic: 7.98 us -> 0 us
    pallas_call x0 -> x1, Pallas kernels: none -> 60.1 us  [local(): pl.pallas_call(functools.partial(kernel, nf, nh, tile_mask.shape[0]), out...]
    ppermute x4 -> x0, waiting for transfers between devices: 45.4 us -> none  [the longest x2 45.4 us: from_behind(): return lax.ppermute(block, axis, route)]
    dot_general x11 -> x0, matrix products: 36.8 us -> none  [the longest x1 5.26 us: local(): jnp.einsum('hts,thd->shd', weights, grads3, preferred_element_type=jnp.fl...]
    ppermute x4 -> x0, starting transfers between devices: 10.9 us -> none  [the longest x2 5.26 us: from_behind(): return lax.ppermute(block, axis, route)]
    all_to_all x1 -> x0, local copies, waits for them, and re-layouts: 7.9 us -> none  [local(): lax.all_to_all(upstream, 'frame', split_axis=1, concat_axis=0, tiled=True)]
    unnamed x39 -> x18, local copies, waits for them, and re-layouts: 17 us -> 9.79 us
    all_to_all x1 -> x0, starting transfers between devices: 5.35 us -> none  [local(): lax.all_to_all(upstream, 'frame', split_axis=1, concat_axis=0, tiled=True)]
    another operation x2 -> x0, local copies, waits for them, and re-layouts: 4.92 us -> none  [local(): jnp.stack([grad_keys, grad_values])]
  transfers between devices with their start and end apart: 7 -> 0, of which waited for: 2 -> 0; matrix products, arithmetic and copies ran while one was open for 43% -> 0% of each run, Pallas kernels for 0% -> 0%
where the time goes in v1:
time: 71 us; the launch traced here: 70.6 us
  Pallas kernels  60.1 us (85%)
  local copies, waits for them, and re-layouts  9.79 us (14%)
    pallas_call x1, Pallas kernels, local(): pl.pallas_call(functools.partial(kernel, nf, nh, tile_mask.shape[0]), out...  60.1 us
    unnamed x18, local copies, waits for them, and re-layouts  9.79 us

profile of v1, /device:TPU:9, one launch (start us, length us, event | category | flops | bytes accessed | tf_op | source)
XLA Modules:
  0.0 70.6 jit_solution(6844779497020044973)
XLA Ops:
  0.6 1.4 %copy.13.tm_ref = s32[16,5]{1,0:T(8,128)} copy(s32[16,5]{0,1:T(8,128)} %param.11) | data formatting | bytes 640 | tf_op args[5]
  2.0 60.1 %shard_map.117 = (bf16[512,256]{1,0:T(8,128)(2,1)}, bf16[512,1280]{1,0:T(8,128)(2,1)}, bf16[512,256]{1,0:T(8,128)(2,1)}, bf16[512,256]{1,0:T(8,128)(2,1)}, bf16[...) custom-call(bf16[512,256]{1,0:T(8,128)(2,1)} %q_hbm.1, bf16[512,256]{1,0:T(8,128)(2,1)} %k_hbm.1, ...), custom_call_target="tpu_custom_call" | custom-call | tf_op jit(solution)/shard_map/pallas_call | solution.py:363
  62.1 0.0 copy-start.4
  62.2 0.0 copy-start.3
  62.2 1.7 %copy.21 = bf16[512,256]{1,0:T(8,128)(2,1)} copy(bf16[512,256]{1,0:T(8,128)(2,1)} %get-tuple-element.14) | data formatting | bytes 524288
  63.9 0.0 copy-start.2
  63.9 0.0 copy-start.1
  63.9 0.0 copy-start
  63.9 2.6 %copy.22 = bf16[512,1280]{1,0:T(8,128)(2,1)} copy(bf16[512,1280]{1,0:T(8,128)(2,1)} %get-tuple-element.15) | data formatting | bytes 2621440
  66.5 0.0 copy-done.4
  66.5 0.7 copy.23
  67.2 0.0 copy-done.3
  67.2 0.7 copy.24
  67.9 0.0 copy-done.2
  67.9 0.7 copy.25
  68.6 0.0 copy-done.1
  68.6 0.7 copy.26
  69.3 0.0 copy-done
  69.3 1.3 %copy.27 = f32[2,2,320,320]{3,2,1,0:T(8,128)} copy(f32[2,2,320,320]{3,2,1,0:T(8,128)S(1)} %copy-done) | data formatting | bytes 3276800
Async XLA Ops:
  62.1 4.4 %copy-start.4 = (bf16[512,256]{1,0:T(8,128)(2,1)S(1)}, bf16[512,256]{1,0:T(8,128)(2,1)}, u32[]{:S(2)}) copy-start(bf16[512,256]{1,0:T(8,128)(2,1)} %get-tuple-element.16) | copy-start | bytes 786436
  62.2 5.1 %copy-start.3 = (bf16[512,256]{1,0:T(8,128)(2,1)S(1)}, bf16[512,256]{1,0:T(8,128)(2,1)}, u32[]{:S(2)}) copy-start(bf16[512,256]{1,0:T(8,128)(2,1)} %get-tuple-element.17) | copy-start | bytes 786436
  63.9 4.0 %copy-start.2 = (bf16[512,256]{1,0:T(8,128)(2,1)S(1)}, bf16[512,256]{1,0:T(8,128)(2,1)}, u32[]{:S(2)}) copy-start(bf16[512,256]{1,0:T(8,128)(2,1)} %get-tuple-element.18) | copy-start | bytes 786436
  63.9 4.7 %copy-start.1 = (f32[2,2,128,128]{3,2,1,0:T(8,128)S(1)}, f32[2,2,128,128]{3,2,1,0:T(8,128)}, u32[]{:S(2)}) copy-start(f32[2,2,128,128]{3,2,1,0:T(8,128)} %get-tuple-element.19) | copy-start | bytes 786436
  63.9 5.4 %copy-start = (f32[2,2,320,320]{3,2,1,0:T(8,128)S(1)}, f32[2,2,320,320]{3,2,1,0:T(8,128)}, u32[]{:S(2)}) copy-start(f32[2,2,320,320]{3,2,1,0:T(8,128)} %get-tuple-element.20) | copy-start | bytes 4915204

commit v2 on v1

--- a/solution.py
+++ b/solution.py
@@ -30,10 +30,10 @@
 def kernel(
     nf, nh, tiles_all,
     q_hbm, k_hbm, v_hbm, w_hbm, wc_hbm, up_hbm, tm_ref,
-    att_o, proj_o, dq_o, dk_o, dv_o, gl_o, gr_o,
+    att_o, proj_o, dq_o, dk_o, dv_o, grad_o,
     qv, kext, vext, wv, upb, wcols, attall, wts, attT, ga, gaT,
     kT, vT, dkacc, dvacc, ghs, ghr, outs, projv, pa, sa, pb, sb, rb,
-    load_sem, up_sem, halo_s, halo_r, w_s, w_r, fw_s, fw_r, at_s, at_r,
+    load_sem, up_sem, halo_s, halo_r, w_s, w_r, tw_s, tw_r, fw_s, fw_r, at_s, at_r,
     sa_s, sa_r, rb_s, rb_r, gh_s, gh_r, out_sem,
 ):
     f = lax.axis_index("frame")
@@ -45,7 +45,7 @@
     tok, hw = qv.shape
     heads = hw // HD
     qt = tok // TILE
-    win = tm_ref.shape[1]
+    win = tm_ref.shape[0]
     reach = (win - 1) // 2
     halo = reach * TILE
     span = win * TILE
@@ -101,22 +101,25 @@
     has_next = f < nf - 1
     has_prev = f > 0
 
-    @pl.when(has_next)
-    def _():
-        for which in range(2):
+    for which in range(2):
+        @pl.when(has_next)
+        def _():
             halo_copy(0, which).start()
 
-    @pl.when(has_prev)
-    def _():
-        for which in range(2):
+        @pl.when(has_prev)
+        def _():
             halo_copy(1, which).start()
 
     my_rows = pl.ds(pl.multiple_of(core * half, half), half)
+    quarter = half // 2
+    upper_half = lax.div(f, nf // 2)
+    other = lax.rem(f + nf // 2, nf)
+    my_part = pl.ds(pl.multiple_of(core * half + upper_half * quarter, quarter), quarter)
     w_copies = []
     for d in range(1, nh):
         j = lax.rem(hd + d, nh)
         cp = pltpu.make_async_remote_copy(
-            src_ref=w_block(j, my_rows), dst_ref=wcols.at[hd, my_rows],
+            src_ref=w_block(j, my_part), dst_ref=wcols.at[hd, my_part],
             send_sem=w_s.at[d], recv_sem=w_r.at[d],
             device_id=(f, j), device_id_type=MESH)
         cp.start()
@@ -143,18 +146,16 @@
     for cp in loads[1:]:
         cp.wait()
 
-    @pl.when(has_prev)
-    def _():
-        for which in range(2):
+    def halo_arrived(which):
+        @pl.when(has_prev)
+        def _():
             halo_copy(0, which).wait_recv()
 
-    @pl.when(has_next)
-    def _():
-        for which in range(2):
+        @pl.when(has_next)
+        def _():
             halo_copy(1, which).wait_recv()
 
-    kT[...] = kext[...].T
-    vT[...] = vext[...].T
+    halo_arrived(0)
 
     def hcols(h):
         return pl.ds(h * HD, HD)
@@ -169,14 +170,21 @@
             for o in range(win):
                 b = tile + o - reach
                 inside = jnp.where(jnp.logical_and(b >= 0, b < tiles_all), 1.0, 0.0)
-                m = tm_ref[tile, o].astype(F32) * inside
+                m = tm_ref[o, tile].astype(F32) * inside
                 parts.append(s[o * TILE:(o + 1) * TILE] * (m * scale) + (m * 1e30 - 1e30))
             s = jnp.concatenate(parts, axis=0)
             p = jnp.exp(s - jnp.max(s, axis=0, keepdims=True))
             total = jnp.sum(p, axis=0, keepdims=True)
             wt = (p * (1.0 / total)).astype(BF16)
             wts[h * qt + i] = wt
-            attT[hcols(h), rows] = dot(vT[hcols(h), keys], wt).astype(BF16)
+    kT[...] = kext[...].T
+    halo_arrived(1)
+    vT[...] = vext[...].T
+    for h in range(heads):
+        for i in range(qt):
+            rows = pl.ds(i * TILE, TILE)
+            keys = pl.ds(i * TILE, span)
+            attT[hcols(h), rows] = dot(vT[hcols(h), keys], wts[h * qt + i]).astype(BF16)
     attall[hd] = attT[...].T
 
     att_out = pltpu.make_async_copy(attall.at[hd], att_o, out_sem.at[0])
@@ -189,6 +197,17 @@
             device_id=(f, lax.rem(hd + d, nh)), device_id_type=MESH)
         cp.start()
         at_copies.append(cp)
+
+    tw_copies = []
+    for d in range(1, nh):
+        w_copies[d - 1].wait_recv()
+        s = lax.rem(hd + nh - d, nh)
+        cp = pltpu.make_async_remote_copy(
+            src_ref=wcols.at[s, my_part], dst_ref=wcols.at[s, my_part],
+            send_sem=tw_s.at[d], recv_sem=tw_r.at[d],
+            device_id=(other, hd), device_id_type=MESH)
+        cp.start()
+        tw_copies.append(cp)
 
     order = [*range(1, chips), 0]
     sa_copies = {}
@@ -268,7 +287,7 @@
 
     fw_copies = []
     for d in range(1, nh):
-        w_copies[d - 1].wait_recv()
+        tw_copies[d - 1].wait_recv()
         s = lax.rem(hd + nh - d, nh)
         cp = pltpu.make_async_remote_copy(
             src_ref=wcols.at[s, my_rows], dst_ref=wcols.at[s, my_rows],
@@ -276,6 +295,25 @@
             device_id=(sib, hd), device_id_type=MESH)
         cp.start()
         fw_copies.append(cp)
+
+    grad = pb[...]
+    for d in range(1, chips):
+        rb_copies[d].wait_recv()
+        grad = grad + rb[d].astype(F32)
+    pb[...] = grad
+    grad_out = pltpu.make_async_copy(pb, grad_o, out_sem.at[5])
+    grad_out.start()
+
+    at_copies_all = at_copies
+    acc = dot(attall[hd], wcols[hd])
+    for d in range(1, nh):
+        s = lax.rem(hd + nh - d, nh)
+        at_copies_all[d - 1].wait_recv()
+        fw_copies[d - 1].wait_recv()
+        acc = acc + dot(attall[s], wcols[s])
+    projv[...] = acc.astype(BF16)
+    proj_out = pltpu.make_async_copy(projv, proj_o, out_sem.at[4])
+    proj_out.start()
 
     @pl.when(has_prev)
     def _():
@@ -295,46 +333,40 @@
     dk_out.start()
     dv_out.start()
 
-    grad = pb[...]
-    for d in range(1, chips):
-        rb_copies[d].wait_recv()
-        grad = grad + rb[d].astype(F32)
-    for h in range(heads):
-        for n in range(cb // CB):
+    for cp in (*w_copies, *tw_copies, *fw_copies, *at_copies, *sa_copies.values(), *rb_copies.values()):
+        cp.wait_send()
+
+    @pl.when(has_next)
+    def _():
+        for which in range(2):
+            halo_copy(0, which).wait_send()
+        gh_copy(0).wait_send()
+
+    @pl.when(has_prev)
+    def _():
+        for which in range(2):
+            halo_copy(1, which).wait_send()
+        gh_copy(1).wait_send()
+
+    for cp in (att_out, dq_out, dk_out, dv_out, proj_out, grad_out):
+        cp.wait()
+
+
+def finish(*refs):
+    sources, grad, results, gl_o, gr_o, sem = refs[:5], refs[5], refs[6:11], *refs[11:]
+    copies = [
+        pltpu.make_async_copy(a, b, sem.at[n]) for n, (a, b) in enumerate(zip(sources, results))]
+    for cp in copies:
+        cp.start()
+    for h in range(grad.shape[0] // HD):
+        for n in range(grad.shape[1] // CB):
             block = grad[h * HD:(h + 1) * HD, n * CB:(n + 1) * CB]
             trace = jnp.sum(jnp.sum(block * block, axis=0, keepdims=True), axis=1, keepdims=True)
             inverse = 1.0 / (trace + epsilon)
             small = block.astype(BF16)
             gl_o[h, n] = dot_nt(small, small) * (inverse * HD)
             gr_o[h, n] = dot(block.T.astype(BF16), small) * (inverse * CB)
-
-    at_copies_all = at_copies
-    acc = dot(attall[hd], wcols[hd])
-    for d in range(1, nh):
-        s = lax.rem(hd + nh - d, nh)
-        at_copies_all[d - 1].wait_recv()
-        fw_copies[d - 1].wait_recv()
-        acc = acc + dot(attall[s], wcols[s])
-    projv[...] = acc.astype(BF16)
-    proj_out = pltpu.make_async_copy(projv, proj_o, out_sem.at[4])
-    proj_out.start()
-
-    for cp in (*w_copies, *fw_copies, *at_copies, *sa_copies.values(), *rb_copies.values()):
-        cp.wait_send()
-
-    @pl.when(has_next)
-    def _():
-        for which in range(2):
-            halo_copy(0, which).wait_send()
-        gh_copy(0).wait_send()
-
-    @pl.when(has_prev)
-    def _():
-        for which in range(2):
-            halo_copy(1, which).wait_send()
-        gh_copy(1).wait_send()
-
-    for cp in (att_out, dq_out, dk_out, dv_out, proj_out):
+    for cp in copies:
         cp.wait()
 
 
@@ -360,7 +392,7 @@
     anywhere = pl.BlockSpec(memory_space=pl.ANY)
     vmem = pl.BlockSpec(memory_space=pltpu.VMEM)
     dma = pltpu.SemaphoreType.DMA
-    return pl.pallas_call(
+    *plain, grad = pl.pallas_call(
         functools.partial(kernel, nf, nh, tile_mask.shape[0]),
         out_shape=(
             jax.ShapeDtypeStruct((tok, hw), BF16),
@@ -368,11 +400,10 @@
             jax.ShapeDtypeStruct((tok, hw), BF16),
             jax.ShapeDtypeStruct((tok, hw), BF16),
             jax.ShapeDtypeStruct((tok, hw), BF16),
-            jax.ShapeDtypeStruct((heads, cb // CB, HD, HD), F32),
-            jax.ShapeDtypeStruct((heads, cb // CB, CB, CB), F32),
+            jax.ShapeDtypeStruct((hw, cb), F32),
         ),
         in_specs=[anywhere] * 6 + [pl.BlockSpec(memory_space=pltpu.SMEM)],
-        out_specs=(anywhere,) * 5 + (vmem, vmem),
+        out_specs=(anywhere,) * 6,
         scratch_shapes=[
             pltpu.VMEM((tok, hw), BF16),
             pltpu.VMEM((ext, hw), BF16),
@@ -404,14 +435,27 @@
             dma((nh,)), dma((nh,)),
             dma((nh,)), dma((nh,)),
             dma((nh,)), dma((nh,)),
+            dma((nh,)), dma((nh,)),
             dma((chips,)), dma((chips,)),
             dma((chips,)), dma((chips,)),
             dma((2,)), dma((2,)),
-            dma((5,)),
+            dma((6,)),
         ],
         compiler_params=pltpu.CompilerParams(
             collective_id=0, has_side_effects=True, vmem_limit_bytes=56 * 1024 * 1024),
-    )(query_states, key_states, value_states, out_weight, w_in, up_in, tile_mask)
+    )(query_states, key_states, value_states, out_weight, w_in, up_in, tile_mask.T)
+    return pl.pallas_call(
+        finish,
+        out_shape=(
+            *(jax.ShapeDtypeStruct(x.shape, x.dtype) for x in plain),
+            jax.ShapeDtypeStruct((heads, cb // CB, HD, HD), F32),
+            jax.ShapeDtypeStruct((heads, cb // CB, CB, CB), F32),
+        ),
+        in_specs=[anywhere] * 5 + [vmem],
+        out_specs=(anywhere,) * 5 + (vmem, vmem),
+        scratch_shapes=[dma((5,))],
+        compiler_params=pltpu.CompilerParams(vmem_limit_bytes=60 * 1024 * 1024),
+    )(*plain, grad)
 
 
 def solution(mesh):

time: 71 us -> 139 us (1.96)
  Pallas kernels: 60.1 us -> 138 us
  local copies, waits for them, and re-layouts: 9.79 us -> 0 us
    pallas_call x0 -> x1, Pallas kernels: none -> 75.1 us  [local(): pl.pallas_call(finish, out_shape=(*(jax.ShapeDtypeStruct(x.shape, x.dtype...]
    unnamed x18 -> x0, local copies, waits for them, and re-layouts: 9.79 us -> none
    pallas_call x1, Pallas kernels: 60.1 us -> 63 us  [local(): pl.pallas_call(functools.partial(kernel, nf, nh, tile_mask.shape[0]), out...]
where the time goes in v2:
time: 139 us
  Pallas kernels  138 us (99%)
    pallas_call x1, Pallas kernels, local(): pl.pallas_call(finish, out_shape=(*(jax.ShapeDtypeStruct(x.shape, x.dtype...  75.1 us
    pallas_call x1, Pallas kernels, local(): pl.pallas_call(functools.partial(kernel, nf, nh, tile_mask.shape[0]), out...  63 us

profile of v2, /device:TPU:9, one launch (start us, length us, event | category | flops | bytes accessed | tf_op | source)
XLA Modules:
  0.0 138.9 jit_solution(7081133692438906202)
XLA Ops:
  0.6 63.0 %shard_map.117 = (bf16[512,256]{1,0:T(8,128)(2,1)}, bf16[512,1280]{1,0:T(8,128)(2,1)}, bf16[512,256]{1,0:T(8,128)(2,1)}, bf16[512,256]{1,0:T(8,128)(2,1)}, bf16[512,256]{1,0:T(8,128)(2,1)}, /*index=5*/f32[256,640]{1,0:T(8,128)}) custom-call(bf16[512,256]{1,0:T(8,128)(2,1)} %q_hbm.1, bf16[512,256]{1,0:T(8,128)(2,1)} %k_hbm.1, bf16[512,256]{1,0:T(8,128)(2,1)} %v_hbm.1, ...), custom_call_target="tpu_custom_call" | custom-call | tf_op jit(solution)/shard_map/pallas_call | solution.py:395
  63.6 75.1 %shard_map.118 = (bf16[512,256]{1,0:T(8,128)(2,1)}, bf16[512,1280]{1,0:T(8,128)(2,1)}, bf16[512,256]{1,0:T(8,128)(2,1)}, bf16[512,256]{1,0:T(8,128)(2,1)}, bf16[...) custom-call(bf16[512,256]{1,0:T(8,128)(2,1)} %get-tuple-element.13.refs_0_, ...), custom_call_target="tpu_custom_call" | custom-call | tf_op jit(solution)/shard_map/pallas_call | solution.py:447

commit v3 on v2

--- a/solution.py
+++ b/solution.py
@@ -353,11 +353,20 @@
 
 
 def finish(*refs):
-    sources, grad, results, gl_o, gr_o, sem = refs[:5], refs[5], refs[6:11], *refs[11:]
+    sources, grad_hbm, results, gl_o, gr_o = refs[:5], refs[5], refs[6:11], refs[11], refs[12]
+    held, grad, in_sem, sem = refs[13:18], refs[18], refs[19], refs[20]
+    grad_in = pltpu.make_async_copy(grad_hbm, grad, in_sem.at[5])
+    grad_in.start()
+    ins = [
+        pltpu.make_async_copy(a, b, in_sem.at[n]) for n, (a, b) in enumerate(zip(sources, held))]
     copies = [
-        pltpu.make_async_copy(a, b, sem.at[n]) for n, (a, b) in enumerate(zip(sources, results))]
-    for cp in copies:
-        cp.start()
+        pltpu.make_async_copy(a, b, sem.at[n]) for n, (a, b) in enumerate(zip(held, results))]
+    for cp in ins:
+        cp.start()
+    for before, after in zip(ins, copies):
+        before.wait()
+        after.start()
+    grad_in.wait()
     for h in range(grad.shape[0] // HD):
         for n in range(grad.shape[1] // CB):
             block = grad[h * HD:(h + 1) * HD, n * CB:(n + 1) * CB]
@@ -451,9 +460,14 @@
             jax.ShapeDtypeStruct((heads, cb // CB, HD, HD), F32),
             jax.ShapeDtypeStruct((heads, cb // CB, CB, CB), F32),
         ),
-        in_specs=[anywhere] * 5 + [vmem],
+        in_specs=[anywhere] * 6,
         out_specs=(anywhere,) * 5 + (vmem, vmem),
-        scratch_shapes=[dma((5,))],
+        scratch_shapes=[
+            *(pltpu.VMEM(x.shape, x.dtype) for x in plain),
+            pltpu.VMEM(grad.shape, F32),
+            dma((6,)),
+            dma((5,)),
+        ],
         compiler_params=pltpu.CompilerParams(vmem_limit_bytes=60 * 1024 * 1024),
     )(*plain, grad)
 

time: 139 us -> 68.4 us (0.49)
  Pallas kernels: 138 us -> 67.4 us
    pallas_call x1, Pallas kernels: 75.1 us -> 4.36 us  [local(): pl.pallas_call(finish, out_shape=(*(jax.ShapeDtypeStruct(x.shape, x.dtype...]
where the time goes in v3:
time: 68.4 us; the launch traced here: 68.2 us
  Pallas kernels  67.4 us (99%)
  between operations  0.8 us (1%)
    pallas_call x1, Pallas kernels, local(): pl.pallas_call(functools.partial(kernel, nf, nh, tile_mask.shape[0]), out...  63 us
    pallas_call x1, Pallas kernels, local(): pl.pallas_call(finish, out_shape=(*(jax.ShapeDtypeStruct(x.shape, x.dtype...  4.36 us

profile of v3, /device:TPU:9, one launch (start us, length us, event | category | flops | bytes accessed | tf_op | source)
XLA Modules:
  0.0 68.2 jit_solution(15854596033585827876)
XLA Ops:
  0.6 63.0 %shard_map.117 = (bf16[512,256]{1,0:T(8,128)(2,1)}, bf16[512,1280]{1,0:T(8,128)(2,1)}, bf16[512,256]{1,0:T(8,128)(2,1)}, bf16[512,256]{1,0:T(8,128)(2,1)}, bf16[512,256]{1,0:T(8,128)(2,1)}, /*index=5*/f32[256,640]{1,0:T(8,128)}) custom-call(bf16[512,256]{1,0:T(8,128)(2,1)} %q_hbm.1, bf16[512,256]{1,0:T(8,128)(2,1)} %k_hbm.1, bf16[512,256]{1,0:T(8,128)(2,1)} %v_hbm.1, ...), custom_call_target="tpu_custom_call" | custom-call | tf_op jit(solution)/shard_map/pallas_call | solution.py:404
  63.6 4.4 %shard_map.118 = (bf16[512,256]{1,0:T(8,128)(2,1)}, bf16[512,1280]{1,0:T(8,128)(2,1)}, bf16[512,256]{1,0:T(8,128)(2,1)}, bf16[512,256]{1,0:T(8,128)(2,1)}, bf16[...) custom-call(bf16[512,256]{1,0:T(8,128)(2,1)} %get-tuple-element.13.refs_0_, ...), custom_call_target="tpu_custom_call" | custom-call | tf_op jit(solution)/shard_map/pallas_call | solution.py:456
